TPU v7x, 32 devices: a whole 2x2x4 slice. The times are simulated.
32 devices in a mesh: col: 8 (over z, core), tile: 4 (over y, x).
Axes of the slice: x: 2, y: 2, z: 4, core: 2. Of those that a mesh axis runs over, the one named last changes fastest.
Arguments:
- boundary: bfloat16 [8, 1024, 4, 1024], P('col', 'tile'), may hold values from -6 to 6
- row_tensors: bfloat16 [8, 4, 4, 4, 4], P('col'), may hold values from -3 to 3
- sketch_bond: bfloat16 [8, 1024, 1024], P('col', 'tile'), may hold values from -0.1875 to 0.1875
- sketch_phys: bfloat16 [8, 4, 4, 1024], P('col'), may hold values from -6 to 6
- edge_factor: bfloat16 [1024, 4, 1024], P('tile'), may hold values from -0.09375 to 0.09375
- closing: float32 [8, 4], P('col'), may hold values from 0.2 to 2
- left_edge: float32 [1024], replicated, may hold values from -6 to 6
Outputs:
- new_boundary: bfloat16 [8, 1024, 4, 1024], P('col', 'tile')
- envs: float32 [8, 1024], P('col', 'tile')
All inputs are finite; a program needn't handle non-finite values.
Results may differ from a plain program's by a relative error of at most 0.012.
The roundings to bfloat16 on the way count: a program that leaves them out, or rounds other values in their place, can miss the bound.
Values may be sent and summed in bfloat16 or wider, within the bound.
No kernel may reach another device: no remote copies, remote signals or barrier semaphores. Data moves between devices by JAX's collectives and lax.ppermute only.
A program may use at most 128 MiB of HBM per device.

v0:
```python
import jax
import jax.numpy as jnp
from jax import lax
from jax.sharding import PartitionSpec as P

GRAM_SHIFT = 0.001


def passed_along(block, axis, distance):
    devices = range(lax.axis_size(axis))
    route = [(i - distance, i) for i in devices if i - distance in devices]
    return lax.ppermute(block, axis, route)


def local(boundary, row_tensors, sketch_bond, sketch_phys, edge_factor, closing, left_edge):
    highest = lax.Precision.HIGHEST
    own_site = boundary[0]
    row_tensor = row_tensors[0].astype(jnp.float32)
    bond_sketch = sketch_bond[0]
    phys_map = jnp.einsum(
        "lurd,ldk->urk", row_tensor, sketch_phys[0].astype(jnp.float32), precision=highest
    )
    local_rows = own_site.shape[0]
    legs = own_site.shape[1]
    width = own_site.shape[2]
    sketched = jnp.einsum(
        "bua,ka->buk",
        own_site,
        lax.all_gather(bond_sketch, "tile", axis=0, tiled=True),
        preferred_element_type=jnp.float32,
    )
    range_rows = jnp.sum(sketched[:, :, None, :] * phys_map[None], axis=1)
    range_flat = range_rows.reshape(local_rows * legs, width)
    gram_local = jnp.dot(range_flat.T, range_flat, precision=highest)
    gram_total = lax.psum(gram_local, "tile") + GRAM_SHIFT * jnp.eye(width, dtype=jnp.float32)
    lower_factor = jnp.linalg.cholesky(gram_total)
    basis = jax.scipy.linalg.solve_triangular(lower_factor, range_flat.T, lower=True).T
    basis = basis.astype(jnp.bfloat16).reshape(local_rows, legs, width)
    arrived = passed_along(basis, "col", 1)
    first_column = lax.axis_index("col") == 0
    left_basis = jnp.where(first_column, edge_factor, arrived)
    basis_cols = lax.all_to_all(basis, "tile", split_axis=2, concat_axis=0, tiled=True)
    matching = basis_cols
    right_part = jnp.einsum(
        "bua,brk->aurk",
        lax.all_gather(own_site, "tile", axis=0, tiled=True),
        matching,
        preferred_element_type=jnp.float32,
    )
    absorbed = jnp.einsum("aurk,lurd->aldk", right_part, row_tensor, precision=highest)
    matching = absorbed
    new_site = jnp.einsum(
        "alc,aldk->kdc",
        lax.all_gather(left_basis, "tile", axis=0, tiled=True).astype(jnp.float32),
        matching,
        precision=highest,
    )
    new_site = new_site.astype(jnp.bfloat16)
    transfer_rows = jnp.einsum(
        "kdc,d->kc", new_site.astype(jnp.float32), closing[0], precision=highest
    ).astype(jnp.bfloat16)
    scale = jnp.sqrt(jnp.float32(width))
    column_count = lax.axis_size("col")
    share = transfer_rows.shape[0]
    transfer_local = transfer_rows.astype(jnp.float32)

    def relay_split(turn_index, current):
        incoming = passed_along(current, "col", 1)
        incoming_whole = lax.all_gather(incoming, "tile", axis=0, tiled=True)
        incoming_whole = jnp.where(first_column, left_edge, incoming_whole)
        weighted = jnp.dot(transfer_local, incoming_whole, precision=highest)
        squares = lax.psum(jnp.sum(weighted * weighted), "tile")
        return weighted * scale / jnp.sqrt(squares + 1e-06)

    env_local = lax.fori_loop(0, column_count, relay_split, jnp.zeros((share,), jnp.float32))
    return (new_site[None], env_local[None])


def solution(mesh):
    in_specs = (
        P("col", "tile", None, None),
        P("col", None, None, None, None),
        P("col", "tile", None),
        P("col", None, None, None),
        P("tile", None, None),
        P("col", None),
        P(),
    )
    out_specs = (P("col", "tile", None, None), P("col", "tile"))
    return jax.shard_map(local, mesh=mesh, in_specs=in_specs, out_specs=out_specs, check_vma=False)
```

profile of v0, /device:TPU:8, one launch (start us, length us, event | category | flops | bytes accessed | tf_op | source)
XLA Modules:
  0.0 937.5 jit_solution(1390344696685670137)
XLA Ops:
  9.1 37.2 %all-gather.12.cloned.1.call-done = bf16[1,1024,1024]{2,1,0:T(8,128)(2,1)} async-done(((bf16[1,256,1024]{2,1,0:T(8,128)(2,1)}), bf16[1,1024,1024]{2,1,0:T(8,128)(2,1)}) %all-gather.12.cloned.1.call-update) | async-done | bytes 2097168 | tf_op jit(solution)/shard_map/all_gather | solution.py:29
  54.5 15.1 %convolution_bitcast_fusion.1 = f32[1024,1024]{0,1:T(8,128)} fusion(f32[256,4,1024]{2,0,1:T(8,128)S(1)} %multiply_reduce_fusion.1), kind=kOutput, calls=%fused_computation.23 | convolution fusion | flops 12884901888 | bytes 8388608 | tf_op jit(solution)/shard_map/dot_general | solution.py:34
  70.9 6.8 copy.190
  77.7 5.3 reshape.87
  83.0 5.4 copy.191
  88.4 85.2 %all-reduce.3.cloned.1.call-done = f32[1024,1024]{0,1:T(8,128)} async-done(((f32[1024,1024]{0,1:T(8,128)}), f32[1024,1024]{0,1:T(8,128)}) %all-reduce.3.cloned.1.call-update) | async-done | bytes 4194320 | tf_op jit(solution)/shard_map/psum | solution.py:35
  178.4 5.4 copy.173
  183.8 5.6 fusion.10
  191.4 11.7 %cholesky.222 = f32[128,128]{1,0:T(8,128)S(1)} custom-call(f32[128,128]{1,0:T(8,128)S(1)} %cholesky.577), custom_call_target="Cholesky" | custom-call | tf_op jit(solution)/shard_map/jit(cholesky)/cholesky | solution.py:36
  203.2 9.8 %custom-call.63 = f32[1,128,128]{1,2,0:T(8,128)S(1)} custom-call(f32[1,128,128]{2,1,0:T(8,128)S(1)} %get-tuple-element.142), custom_call_target="InvertDiagBlocksLowerTriangular" | custom-call | tf_op jit(solution)/shard_map/jit(cholesky)/cholesky | solution.py:36
  216.4 11.7 %cholesky.243 = f32[128,128]{1,0:T(8,128)S(1)} custom-call(f32[128,128]{1,0:T(8,128)S(1)} %cholesky.581), custom_call_target="Cholesky" | custom-call | tf_op jit(solution)/shard_map/jit(cholesky)/cholesky | solution.py:36
  228.4 9.8 %custom-call.64 = f32[1,128,128]{1,2,0:T(8,128)S(1)} custom-call(f32[1,128,128]{2,1,0:T(8,128)S(1)} %get-tuple-element.140), custom_call_target="InvertDiagBlocksLowerTriangular" | custom-call | tf_op jit(solution)/shard_map/jit(cholesky)/cholesky | solution.py:36
  243.7 11.7 %cholesky.466 = f32[128,128]{1,0:T(8,128)S(1)} custom-call(f32[128,128]{1,0:T(8,128)S(1)} %cholesky.586), custom_call_target="Cholesky" | custom-call | tf_op jit(solution)/shard_map/jit(cholesky)/cholesky | solution.py:36
  256.2 9.8 %custom-call.65 = f32[1,128,128]{1,2,0:T(8,128)S(1)} custom-call(f32[1,128,128]{2,1,0:T(8,128)S(1)} %get-tuple-element.138), custom_call_target="InvertDiagBlocksLowerTriangular" | custom-call | tf_op jit(solution)/shard_map/jit(cholesky)/cholesky | solution.py:36
  270.6 11.7 %cholesky.485 = f32[128,128]{1,0:T(8,128)S(1)} custom-call(f32[128,128]{1,0:T(8,128)S(1)} %cholesky.591), custom_call_target="Cholesky" | custom-call | tf_op jit(solution)/shard_map/jit(cholesky)/cholesky | solution.py:36
  283.1 9.8 %custom-call.66 = f32[1,128,128]{1,2,0:T(8,128)S(1)} custom-call(f32[1,128,128]{2,1,0:T(8,128)S(1)} %get-tuple-element.136), custom_call_target="InvertDiagBlocksLowerTriangular" | custom-call | tf_op jit(solution)/shard_map/jit(cholesky)/cholesky | solution.py:36
  297.2 12.2 %cholesky.504 = f32[128,128]{1,0:T(8,128)S(1)} custom-call(f32[128,128]{1,0:T(8,128)S(1)} %cholesky.596), custom_call_target="Cholesky" | custom-call | tf_op jit(solution)/shard_map/jit(cholesky)/cholesky | solution.py:36
  310.2 9.8 %custom-call.67 = f32[1,128,128]{1,2,0:T(8,128)S(1)} custom-call(f32[1,128,128]{2,1,0:T(8,128)S(1)} %get-tuple-element.134), custom_call_target="InvertDiagBlocksLowerTriangular" | custom-call | tf_op jit(solution)/shard_map/jit(cholesky)/cholesky | solution.py:36
  324.3 11.7 %cholesky.524 = f32[128,128]{1,0:T(8,128)S(1)} custom-call(f32[128,128]{1,0:T(8,128)S(1)} %cholesky.601), custom_call_target="Cholesky" | custom-call | tf_op jit(solution)/shard_map/jit(cholesky)/cholesky | solution.py:36
  336.8 9.8 %custom-call.68 = f32[1,128,128]{1,2,0:T(8,128)S(1)} custom-call(f32[1,128,128]{2,1,0:T(8,128)S(1)} %get-tuple-element.132), custom_call_target="InvertDiagBlocksLowerTriangular" | custom-call | tf_op jit(solution)/shard_map/jit(cholesky)/cholesky | solution.py:36
  350.6 11.7 %cholesky.544 = f32[128,128]{1,0:T(8,128)S(1)} custom-call(f32[128,128]{1,0:T(8,128)S(1)} %cholesky.606), custom_call_target="Cholesky" | custom-call | tf_op jit(solution)/shard_map/jit(cholesky)/cholesky | solution.py:36
  363.1 9.8 %custom-call.69 = f32[1,128,128]{1,2,0:T(8,128)S(1)} custom-call(f32[1,128,128]{2,1,0:T(8,128)S(1)} %get-tuple-element.130), custom_call_target="InvertDiagBlocksLowerTriangular" | custom-call | tf_op jit(solution)/shard_map/jit(cholesky)/cholesky | solution.py:36
  376.7 11.7 %cholesky.562 = f32[128,128]{1,0:T(8,128)S(1)} custom-call(f32[128,128]{1,0:T(8,128)S(1)} %convolution_subtract_fusion.11), custom_call_target="Cholesky" | custom-call | tf_op jit(solution)/shard_map/jit(cholesky)/cholesky | solution.py:36
  398.2 4.9 select_select_fusion
  403.0 23.5 %while.12 = (s32[]{:T(128)}, f32[1024,1024]{0,1:T(8,128)}, s32[8,2]{0,1:T(2,128)S(1)}, f32[8,128,128]{2,1,0:T(8,128)S(1)}, s32[]{:T(128)}) while((s32[]{:T(128)}, f32[1024,1024]{0,1:T(8,128)}, s32[8,2]{0,1:T(2,128)S(1)}, f32[8,128,128]{2,1,0:T(8,128)S(1)}, s32[]{:T(128)}) %tuple.78), condition=%wide.while_cond, body=%wide.while_body.sunk | while | flops 2 | bytes 393321 | solution.py:37
  426.5 79.0 %custom-call.70 = f32[8,128,128]{1,2,0:T(8,128)S(1)} custom-call(f32[8,128,128]{2,1,0:T(8,128)S(1)} %get-tuple-element.37), custom_call_target="InvertDiagBlocksLowerTriangular" | custom-call | tf_op jit(solution)/shard_map/jit(_solve_triangular)/triangular_solve | solution.py:37
  538.8 25.7 %collective-permute-done.1 = bf16[256,4,1024]{2,0,1:T(8,128)(2,1)} collective-permute-done((bf16[256,4,1024]{2,0,1:T(8,128)(2,1)}, bf16[256,4,1024]{2,0,1:T(8,128)(2,1)}, u32[]{:S(2)}, u32[]{:S(2)}) %collective-permute-start.1) | collective-permute-done | bytes 2097184 | tf_op jit(solution)/shard_map/ppermute | solution.py:12
  576.5 46.0 %all-to-all-done = bf16[256,4,1024]{0,1,2:T(4,128)(2,1)S(1)} async-done(((bf16[256,4,1024]{0,1,2:T(4,128)(2,1)}), bf16[256,4,1024]{0,1,2:T(4,128)(2,1)S(1)}, u32[]{:S(2)}, u32[]{:S(2)}) %all-to-all-start) | async-done | bytes 2097184 | tf_op jit(solution)/shard_map/all_to_all | solution.py:42
  627.1 15.8 %convolution_bitcast_fusion = f32[1024,4,4,256,1]{0,3,1,2,4:T(8,128)} fusion(bf16[1024,4,256,1]{2,0,3,1:T(8,128)(2,1)S(1)} %bitcast.199, bf16[1,1024,4,1024]{3,2,0,1:T(4,128)(2,1)} %all-gather.14.cloned.1.call-done), kind=kOutput, calls=%fused_computation.11 | convolution fusion | flops 8589934592 | bytes 27262976 | tf_op jit(solution)/shard_map/bua,brk->aurk/dot_general | solution.py:44
  642.8 44.1 %fusion.7 = f32[1024,4,4,256]{0,2,1,3:T(4,128)} fusion(f32[1024,4,4,256,1]{0,3,1,2,4:T(8,128)} %convolution_bitcast_fusion, bf16[1,4,4,4,4]{4,3,2,1,0:T(4,128)(2,1)S(1)} %copy-done.7), kind=kOutput, calls=%fused_computation.15 | convolution fusion | flops 805306368 | bytes 33554944 | tf_op jit(solution)/shard_map/aurk,lurd->aldk/dot_general | solution.py:50
  686.9 40.7 %bitcast_convert_fusion = bf16[4,256,1024]{2,1,0:T(8,128)(2,1)S(1)} fusion(bf16[1024,4,1024]{2,0,1:T(8,128)(2,1)} %all-gather.10.cloned.1.call-done, f32[1024,4,4,256]{0,2,1,3:T(4,128)} %fusion.7), kind=kOutput, calls=%fused_computation.17 | convolution fusion | flops 51540656128 | bytes 27262976 | tf_op jit(solution)/shard_map/alc,aldk->kdc/dot_general | solution.py:52
  734.7 195.5 %while.13 = (s32[]{:T(128)}, f32[256]{0:T(256)S(1)}, pred[]{:T(512)}, f32[1024]{0:T(1024)S(1)}, f32[256,1024]{1,0:T(8,128)S(1)}, /*index=5*/s32[]{:T(128)}, s32[]{:T(128)}, f32[]{:T(128)}) while((s32[]{:T(128)}, f32[256]{0:T(256)S(1)}, pred[]{:T(512)}, f32[1024]{0:T(1024)S(1)}, f32[256,1024]{1,0:T(8,128)S(1)}, ...), condition=%wide.region_21.22_spmd.clone, body=%wide.region_18.21_spmd.clone.sunk | while | flops 3148036 | bytes 1080492 | solution.py:75
  739.6 8.0 all-gather.5
  749.2 9.6 %psum.17 = f32[]{:T(128)} all-reduce(f32[]{:T(128)} %multiply_reduce_fusion.3), channel_id=1, replica_groups=mesh['col'=8,'tile'=4] {'tile'}, use_global_device_ids=true, to_apply=%region_20.20 | all-reduce | flops 1 | bytes 8 | tf_op jit(solution)/shard_map/while/body/eval_jaxpr/psum | solution.py:72
  764.5 7.1 all-gather.5
  773.2 9.6 %psum.17 = f32[]{:T(128)} all-reduce(f32[]{:T(128)} %multiply_reduce_fusion.3), channel_id=1, replica_groups=mesh['col'=8,'tile'=4] {'tile'}, use_global_device_ids=true, to_apply=%region_20.20 | all-reduce | flops 1 | bytes 8 | tf_op jit(solution)/shard_map/while/body/eval_jaxpr/psum | solution.py:72
  788.5 8.0 all-gather.5
  798.1 9.6 %psum.17 = f32[]{:T(128)} all-reduce(f32[]{:T(128)} %multiply_reduce_fusion.3), channel_id=1, replica_groups=mesh['col'=8,'tile'=4] {'tile'}, use_global_device_ids=true, to_apply=%region_20.20 | all-reduce | flops 1 | bytes 8 | tf_op jit(solution)/shard_map/while/body/eval_jaxpr/psum | solution.py:72
  813.3 7.1 all-gather.5
  822.1 9.6 %psum.17 = f32[]{:T(128)} all-reduce(f32[]{:T(128)} %multiply_reduce_fusion.3), channel_id=1, replica_groups=mesh['col'=8,'tile'=4] {'tile'}, use_global_device_ids=true, to_apply=%region_20.20 | all-reduce | flops 1 | bytes 8 | tf_op jit(solution)/shard_map/while/body/eval_jaxpr/psum | solution.py:72
  837.4 8.0 all-gather.5
  847.0 9.6 %psum.17 = f32[]{:T(128)} all-reduce(f32[]{:T(128)} %multiply_reduce_fusion.3), channel_id=1, replica_groups=mesh['col'=8,'tile'=4] {'tile'}, use_global_device_ids=true, to_apply=%region_20.20 | all-reduce | flops 1 | bytes 8 | tf_op jit(solution)/shard_map/while/body/eval_jaxpr/psum | solution.py:72
  862.2 7.1 all-gather.5
  871.0 9.6 %psum.17 = f32[]{:T(128)} all-reduce(f32[]{:T(128)} %multiply_reduce_fusion.3), channel_id=1, replica_groups=mesh['col'=8,'tile'=4] {'tile'}, use_global_device_ids=true, to_apply=%region_20.20 | all-reduce | flops 1 | bytes 8 | tf_op jit(solution)/shard_map/while/body/eval_jaxpr/psum | solution.py:72
  886.2 8.0 all-gather.5
  895.8 9.6 %psum.17 = f32[]{:T(128)} all-reduce(f32[]{:T(128)} %multiply_reduce_fusion.3), channel_id=1, replica_groups=mesh['col'=8,'tile'=4] {'tile'}, use_global_device_ids=true, to_apply=%region_20.20 | all-reduce | flops 1 | bytes 8 | tf_op jit(solution)/shard_map/while/body/eval_jaxpr/psum | solution.py:72
  911.1 7.1 all-gather.5
  919.9 9.6 %psum.17 = f32[]{:T(128)} all-reduce(f32[]{:T(128)} %multiply_reduce_fusion.3), channel_id=1, replica_groups=mesh['col'=8,'tile'=4] {'tile'}, use_global_device_ids=true, to_apply=%region_20.20 | all-reduce | flops 1 | bytes 8 | tf_op jit(solution)/shard_map/while/body/eval_jaxpr/psum | solution.py:72
  (222 shorter events, 188.9 us)
Async XLA Ops:
  7.2 0.8 copy-start
  7.2 39.2 %all-gather.12.cloned.1.call-start = ((), (), s32[]{:S(2)}) async-start(), calls=%async_computation.3 | async-start | bytes 2621440 | tf_op jit(solution)/shard_map/all_gather | solution.py:29
  7.9 165.7 %all-reduce.3.cloned.1.call-start = ((), (), s32[]{:S(2)}) async-start(), calls=%async_computation.1 | async-start | bytes 8388608 | tf_op jit(solution)/shard_map/psum | solution.py:35
  52.5 1.9 copy-start.3
  69.6 557.4 %all-gather.14.cloned.1.call-start = ((), (), s32[]{:S(2)}) async-start(), calls=%async_computation.4 | async-start | bytes 10485760 | tf_op jit(solution)/shard_map/all_gather | solution.py:46
  70.4 616.6 %all-gather.10.cloned.1.call-start = ((), (), s32[]{:S(2)}) async-start(), calls=%async_computation.2 | async-start | bytes 10485760 | tf_op jit(solution)/shard_map/all_gather | solution.py:54
  189.4 2.0 copy-start.5
  239.3 2.0 copy-start.2
  505.5 4.6 copy-start.4
  536.8 27.7 %collective-permute-start.1 = (bf16[256,4,1024]{2,0,1:T(8,128)(2,1)}, bf16[256,4,1024]{2,0,1:T(8,128)(2,1)}, u32[]{:S(2)}, u32[]{:S(2)}) collective-permute-start(bf16[256,4,1024]{2,0,1:T(8,128)(2,1)} %copy.201), channel_id=1, source_target_pairs={{0,4},{4,8},{8,12},{12,16},{16,20},{20,24},{24,28},{1,5},{5,9},{9,... | collective-permute-start | bytes 6291464 | tf_op jit(solution)/shard_map/ppermute | solution.py:12
  572.9 49.7 %all-to-all-start = ((bf16[256,4,1024]{0,1,2:T(4,128)(2,1)}), bf16[256,4,1024]{0,1,2:T(4,128)(2,1)S(1)}, u32[]{:S(2)}, u32[]{:S(2)}) async-start(bf16[256,4,1024]{0,1,2:T(4,128)(2,1)} %copy.193), calls=%async_computation | async-start | bytes 4194304 | tf_op jit(solution)/shard_map/all_to_all | solution.py:42
  627.0 15.8 %copy-start.7 = (bf16[1,4,4,4,4]{4,3,2,1,0:T(4,128)(2,1)S(1)}, bf16[1,4,4,4,4]{4,3,2,1,0:T(4,128)(2,1)}, u32[]{:S(2)}) copy-start(bf16[1,4,4,4,4]{4,3,2,1,0:T(4,128)(2,1)} %param.10) | copy-start | bytes 1540
  686.9 40.7 %copy-start.9 = (f32[1,4]{1,0:T(1,128)S(1)}, f32[1,4]{1,0:T(1,128)}, u32[]{:S(2)}) copy-start(f32[1,4]{1,0:T(1,128)} %param.14) | copy-start | bytes 52
  731.5 3.2 copy-start.6
  731.8 199.0 %copy-start.1 = (bf16[1,4,4,1024]{3,2,1,0:T(4,128)(2,1)S(1)}, bf16[1,4,4,1024]{3,2,1,0:T(4,128)(2,1)}, u32[]{:S(2)}) copy-start(bf16[1,4,4,1024]{3,2,1,0:T(4,128)(2,1)} %param.12) | copy-start | bytes 98308
  734.7 4.9 collective-permute-start
  759.6 4.9 collective-permute-start
  783.6 4.9 collective-permute-start
  808.5 4.9 collective-permute-start
  832.5 4.9 collective-permute-start
  857.3 4.9 collective-permute-start
  881.4 4.9 collective-permute-start
  906.2 4.9 collective-permute-start
  930.2 0.6 copy-start.8
Sparse Core Ops, SparseCore 0:
  9.9 36.4 all-gather.11
  69.7 103.8 all-reduce.2
  175.6 87.7 all-gather.13
  569.4 105.9 all-gather.9
where the time goes:
time: 947 us; the launch traced here: 938 us
  other arithmetic  274 us (29%)
  waiting for transfers between devices  219 us (23%)
  matrix products  182 us (19%)
  blocking collectives  137 us (14%)
  local copies, waits for them, and re-layouts  77.4 us (8%)
  starting transfers between devices  21.5 us (2%)
  between operations  19.8 us (2%)
    another operation x30, other arithmetic, local(): lower_factor = jnp.linalg.cholesky(gram_total)  168 us
    psum x1, waiting for transfers between devices, local(): lax.psum(gram_local, 'tile')  85.2 us
    another operation x3, other arithmetic, local(): jax.scipy.linalg.solve_triangular(lower_factor, range_flat.T, lower=True)  83.9 us
    psum x8, blocking collectives, relay_split(): squares = lax.psum(jnp.sum(weighted * weighted), 'tile')  76.8 us
    all_gather x8, blocking collectives, relay_split(): incoming_whole = lax.all_gather(incoming, 'tile', axis=0, tiled=True)  60.4 us
    ppermute x9, waiting for transfers between devices, passed_along(): return lax.ppermute(block, axis, route)  49.4 us
    all_to_all x1, waiting for transfers between devices, local(): lax.all_to_all(basis, 'tile', split_axis=2, concat_axis=0, tiled=True)  46 us
    dot_general x1, matrix products, local(): jnp.einsum('aurk,lurd->aldk', right_part, row_tensor, precision=highest)  44.1 us
  transfers between devices with their start and end apart: 14, of which 12 were waited for; matrix products, arithmetic and copies ran while one was open for 47% of the time, Pallas kernels for 0%

commit v1 on v0

--- a/solution.py
+++ b/solution.py
@@ -1,9 +1,21 @@
+import functools
+
 import jax
 import jax.numpy as jnp
 from jax import lax
+from jax.experimental import pallas as pl
+from jax.experimental.pallas import tpu as pltpu
 from jax.sharding import PartitionSpec as P
 
 GRAM_SHIFT = 0.001
+F32 = jnp.float32
+BF16 = jnp.bfloat16
+LANES = 128
+SUB = 8
+VMEM = pltpu.VMEM
+NT = ((1,), (1,))
+NN = ((1,), (0,))
+AXES = ("col", "tile")
 
 
 def passed_along(block, axis, distance):
@@ -12,7 +24,7 @@
     return lax.ppermute(block, axis, route)
 
 
-def local(boundary, row_tensors, sketch_bond, sketch_phys, edge_factor, closing, left_edge):
+def plain(boundary, row_tensors, sketch_bond, sketch_phys, edge_factor, closing, left_edge):
     highest = lax.Precision.HIGHEST
     own_site = boundary[0]
     row_tensor = row_tensors[0].astype(jnp.float32)
@@ -76,6 +88,477 @@
     return (new_site[None], env_local[None])
 
 
+def call(kernel, name, flops, vmem, **kwargs):
+    return pl.pallas_call(
+        kernel,
+        name=name,
+        compiler_params=pltpu.CompilerParams(vmem_limit_bytes=vmem * 2**20),
+        cost_estimate=pl.CostEstimate(flops=int(flops), bytes_accessed=1 << 20, transcendentals=0),
+        **kwargs,
+    )
+
+
+def whole(count):
+    return [pl.BlockSpec(memory_space=VMEM)] * count
+
+
+def scalars(count):
+    return [pl.BlockSpec(memory_space=pltpu.SMEM)] * count
+
+
+def two_parts(x):
+    hi = x.astype(BF16)
+    return hi, (x - hi.astype(F32)).astype(BF16)
+
+
+def dot1(a, b, dims):
+    return lax.dot_general(a, b, (dims, ((), ())), preferred_element_type=F32)
+
+
+def dot3(a, b, dims):
+    (ah, al), (bh, bl) = a, b
+    return dot1(ah, bh, dims) + (dot1(ah, bl, dims) + dot1(al, bh, dims))
+
+
+def spread(x):
+    return jnp.broadcast_to(x, (SUB, LANES))
+
+
+def factor_panel(s):
+    s = dict(s)
+    inv = {}
+    for c in range(SUB):
+        rs = lax.rsqrt(s[c, c])
+        low = {r: s[r, c] * rs for r in range(c + 1, SUB)}
+        for r in range(c + 1, SUB):
+            for q in range(c + 1, r + 1):
+                s[r, q] = s[r, q] - low[r] * low[q]
+        for q in range(c):
+            inv[c, q] = inv[c, q] * rs
+        inv[c, c] = rs
+        for r in range(c + 1, SUB):
+            for q in range(c + 1):
+                term = low[r] * inv[c, q]
+                inv[r, q] = inv[r, q] - term if (r, q) in inv else -term
+    return inv
+
+
+def inverse_factor(block):
+    n = LANES // SUB
+    row = lax.broadcasted_iota(jnp.int32, (SUB, LANES), 0)
+    lane = lax.broadcasted_iota(jnp.int32, (SUB, LANES), 1)
+    zero = jnp.zeros((SUB, LANES), F32)
+    a = [block[SUB * i : SUB * (i + 1), :] for i in range(n)]
+    e = [jnp.where(lane == row + SUB * i, 1.0, 0.0).astype(F32) for i in range(n)]
+    out = []
+    for p in range(n):
+        u, eu = a[p], e[p]
+        cols = [spread(u[:, SUB * p + c : SUB * p + c + 1]) for c in range(SUB)]
+        inv = factor_panel({(r, c): spread(cols[c][r : r + 1, :]) for c in range(SUB) for r in range(c, SUB)})
+        w, we = zero, zero
+        for c in range(SUB):
+            m = zero
+            for r in range(c, SUB):
+                m = jnp.where(row == r, inv[r, c], m)
+            if p < n - 1:
+                w = w + m * spread(u[c : c + 1, :])
+            we = we + m * spread(eu[c : c + 1, :])
+        out.append(we)
+        if p == n - 1:
+            break
+        v, ve = zero, zero
+        for q in range(SUB):
+            m = zero
+            for c in range(q + 1):
+                m = jnp.where(row == c, inv[q, c], m)
+            v = v + m * spread(w[q : q + 1, :])
+            ve = ve + m * spread(we[q : q + 1, :])
+        vs = [spread(v[c : c + 1, :]) for c in range(SUB)]
+        ves = [spread(ve[c : c + 1, :]) for c in range(SUB)]
+        for i in range(p + 1, n):
+            for c in range(SUB):
+                low = spread(a[i][:, SUB * p + c : SUB * p + c + 1]) if c == 0 else lows[c]
+                if c == 0:
+                    lows = [low] + [spread(a[i][:, SUB * p + k : SUB * p + k + 1]) for k in range(1, SUB)]
+                a[i] = a[i] - low * vs[c]
+                e[i] = e[i] - low * ves[c]
+    return jnp.concatenate(out, 0)
+
+
+def sketch_kernel(parts, first, where_ref, map_ref, *refs):
+    bonds, site, refs = refs[:parts], refs[parts], refs[parts + 1 :]
+    legs, share, _ = site.shape
+    size = bonds[0].shape[0]
+    before = () if first else refs[:parts]
+    rows_ref, panels, high, low = refs[0 if first else parts], refs[-2 - parts : -2], refs[-2], refs[-1]
+    for n in range(parts):
+        at = pl.ds(pl.multiple_of(where_ref[n] * size, size), size)
+        sk = [dot1(bonds[n][...], site[u], NT) for u in range(legs)]
+        for r in range(legs):
+            total = sk[0] * map_ref[at, r : r + 1]
+            for u in range(1, legs):
+                total = total + sk[u] * map_ref[at, u * legs + r : u * legs + r + 1]
+            rows_ref[at, r * share : (r + 1) * share] = total
+            hi, lo = two_parts(total)
+            high[at, r * share : (r + 1) * share] = hi
+            low[at, r * share : (r + 1) * share] = lo
+    for j in range(parts):
+        right = (high[j * size : (j + 1) * size, :], low[j * size : (j + 1) * size, :])
+        for i in range(j, parts):
+            left = (high[i * size : (i + 1) * size, :], low[i * size : (i + 1) * size, :])
+            block = dot3(left, right, NT)
+            at = slice((i - j) * size, (i - j + 1) * size)
+            if not first:
+                block = block + before[j][at, :]
+            panels[j][at, :] = block
+
+
+def sketch(where, phys, bonds, site, before):
+    parts = len(bonds)
+    size, width = bonds[0].shape
+    legs, share, _ = site.shape
+    shapes = [jax.ShapeDtypeStruct((width, legs * share), F32)]
+    shapes += [jax.ShapeDtypeStruct((width - j * size, size), F32) for j in range(parts)]
+    out = call(
+        functools.partial(sketch_kernel, parts, not before),
+        "sketch",
+        5e9,
+        48,
+        out_shape=shapes,
+        in_specs=scalars(1) + whole(parts + 2 + len(before)),
+        out_specs=whole(parts + 1),
+        scratch_shapes=[VMEM((width, legs * share), BF16)] * 2,
+    )(where, phys, *bonds, site, *before)
+    return out[0], list(out[1:])
+
+
+def basis_kernel(turn, groups, last, *refs):
+    own, other, refs = refs[0], refs[1], refs[2:]
+    lows, refs = refs[:turn], refs[turn:]
+    highs, refs = refs[:turn], refs[turn:]
+    rests, refs = refs[:turn], refs[turn:]
+    rows, refs = refs[:groups], refs[groups:]
+    size = own.shape[1]
+    half = size // 2
+    s = own[...] + other[...]
+    row = lax.broadcasted_iota(jnp.int32, s.shape, 0)
+    lane = lax.broadcasted_iota(jnp.int32, s.shape, 1)
+    s = s + jnp.where(row == lane, GRAM_SHIFT, 0.0).astype(F32)
+    facing = []
+    for i in range(turn):
+        at = (turn - i - 1) * size
+        below = two_parts(lows[i][at:, :])
+        facing.append((below[0][:size], below[1][:size]))
+        s = s - dot3(below, facing[i], NT)
+    x1 = inverse_factor(s[:half, :half])
+    x1p = two_parts(x1)
+    l21p = two_parts(dot3(two_parts(s[half:size, :half]), x1p, NT))
+    x2 = inverse_factor(s[half:size, half:] - dot3(l21p, l21p, NT))
+    x2p = two_parts(x2)
+    x21 = -dot3(x2p, two_parts(dot3(l21p, x1p, NN)), NN)
+    inv = jnp.concatenate(
+        [jnp.concatenate([x1, jnp.zeros((half, half), F32)], 1), jnp.concatenate([x21, x2], 1)], 0
+    )
+    inv = two_parts(inv)
+    if not last:
+        refs[0][...] = dot3(two_parts(s[size:, :]), inv, NT)
+    for g in range(groups):
+        part = rows[g][...]
+        for i in range(turn):
+            part = part - dot3(facing[i], (highs[i][g], rests[i][g]), NN)
+        hi, lo = two_parts(dot3(inv, two_parts(part), NN))
+        if last:
+            refs[0][g] = hi
+        else:
+            refs[1][g] = hi
+            refs[2][g] = lo
+
+
+def basis_columns(turn, own, other, lows, highs, rests, rows):
+    size = own.shape[1]
+    groups = len(rows)
+    last = own.shape[0] == size
+    cols = jax.ShapeDtypeStruct((groups, size, rows[0].shape[1]), BF16)
+    shapes = [cols] if last else [jax.ShapeDtypeStruct((own.shape[0] - size, size), F32), cols, cols]
+    rows_spec = pl.BlockSpec((size, rows[0].shape[1]), lambda i: (turn, 0))
+    return call(
+        functools.partial(basis_kernel, turn, groups, last),
+        "basis",
+        15e9,
+        56,
+        out_shape=shapes,
+        grid=(1,),
+        in_specs=whole(2 + 3 * turn) + [rows_spec] * groups,
+        out_specs=whole(len(shapes)),
+    )(own, other, *lows, *highs, *rests, *rows)
+
+
+def absorb_kernel(legs, mix_ref, basis_a, basis_b, site_a, site_b, out_ref, held):
+    groups, size, wide = basis_a.shape
+    share = wide // legs
+    step = mix_ref.shape[0] // (legs * legs)
+    for u in range(legs):
+        for r in range(legs):
+            at = slice(r * share, (r + 1) * share)
+            total = None
+            for basis, site in ((basis_a, site_a), (basis_b, site_b)):
+                for g in range(groups):
+                    term = dot1(basis[g, :, at], site[g, u], NN)
+                    total = term if total is None else total + term
+            held[u * legs + r] = total.astype(BF16)
+    block = held.shape[2]
+    for n in range(size // step):
+        rows = slice(n * step, (n + 1) * step)
+        stack = jnp.concatenate([held[m, rows, :] for m in range(legs * legs)], 0)
+        mixed = dot1(mix_ref[...], stack, NN).astype(BF16)
+        for d in range(legs):
+            for l in range(legs):
+                m = (d * legs + l) * step
+                out_ref[0, d * size + n * step : d * size + (n + 1) * step, l * block : (l + 1) * block] = mixed[
+                    m : m + step
+                ]
+
+
+def absorb(mix, basis_a, basis_b, site_a, site_b):
+    groups, size, wide = basis_a.shape
+    _, legs, share, width = site_a.shape
+    parts = width // size
+    site_spec = pl.BlockSpec((groups, legs, share, size), lambda i: (0, 0, 0, i))
+    return call(
+        functools.partial(absorb_kernel, legs),
+        "absorb",
+        15e9,
+        48,
+        out_shape=jax.ShapeDtypeStruct((parts, legs * size, legs * size), BF16),
+        grid=(parts,),
+        in_specs=whole(3) + [site_spec] * 2,
+        out_specs=pl.BlockSpec((1, legs * size, legs * size), lambda i: (i, 0, 0)),
+        scratch_shapes=[VMEM((legs * legs, size, size), BF16)],
+    )(mix, basis_a, basis_b, site_a, site_b)
+
+
+def close_kernel(parts, legs, where_ref, weights, absorbed, *refs):
+    lefts, site_ref, transfer_ref, total = refs[:parts], refs[parts], refs[parts + 1], refs[parts + 2]
+    n = pl.program_id(0)
+
+    @pl.when(n == 0)
+    def _():
+        total[...] = jnp.zeros_like(total)
+
+    for i in range(parts):
+
+        @pl.when(n == i)
+        def _():
+            total[...] += dot1(absorbed[0], lefts[i][...], NT)
+
+    @pl.when(n == parts - 1)
+    def _():
+        size = transfer_ref.shape[0]
+        closed = None
+        for d in range(legs):
+            part = total[d * size : (d + 1) * size, :].astype(BF16)
+            site_ref[d] = part
+            term = part.astype(F32) * weights[d]
+            closed = term if closed is None else closed + term
+        transfer_ref[...] = closed.astype(BF16)
+
+
+def close(where, weights, absorbed, lefts):
+    parts, tall, wide = absorbed.shape
+    legs = weights.shape[0]
+    size, block = tall // legs, lefts[0].shape[0]
+    return call(
+        functools.partial(close_kernel, parts, legs),
+        "close",
+        3e9,
+        48,
+        out_shape=[
+            jax.ShapeDtypeStruct((legs, size, block), BF16),
+            jax.ShapeDtypeStruct((size, block), BF16),
+        ],
+        grid_spec=pltpu.PrefetchScalarGridSpec(
+            num_scalar_prefetch=1,
+            grid=(parts,),
+            in_specs=scalars(1)
+            + [pl.BlockSpec((1, tall, wide), lambda i, where: (where[i], 0, 0))]
+            + whole(parts),
+            out_specs=whole(2),
+            scratch_shapes=[VMEM((tall, block), F32)],
+        ),
+    )(where, weights, absorbed, *lefts)
+
+
+def relay_kernel(parts, info, coming, kept, *refs):
+    transfers, out, weighted = refs[:parts], refs[parts], refs[parts + 1]
+    size, width = transfers[0].shape
+    whole_env = coming[...]
+    first = whole_env.astype(BF16)
+    left = whole_env - first.astype(F32)
+    second = left.astype(BF16)
+    third = (left - second.astype(F32)).astype(BF16)
+    row = lax.broadcasted_iota(jnp.int32, (16, width), 0)
+    grow = lambda v: jnp.broadcast_to(v.astype(F32), (16, width))
+    lhs = jnp.where(row == 0, grow(first), jnp.where(row == 1, grow(second), jnp.where(row == 2, grow(third), 0.0)))
+    lhs = lhs.astype(BF16)
+    for n in range(parts):
+        product = dot1(lhs, transfers[n][...], NT)
+        at = pl.ds(pl.multiple_of(info[n] * size, size), size)
+        weighted[:, at] = jnp.sum(product, axis=0, keepdims=True)
+    w = weighted[...]
+    squares = jnp.sum(w * w, axis=1, keepdims=True)
+    env = w * jnp.sqrt(jnp.float32(width)) / jnp.sqrt(squares + 1e-06)
+    out[...] = jnp.where(info[parts] == 1, env, kept[...])
+
+
+def relay(info, coming, kept, transfers):
+    parts = len(transfers)
+    return call(
+        functools.partial(relay_kernel, parts),
+        "relay",
+        1e8,
+        24,
+        out_shape=jax.ShapeDtypeStruct(kept.shape, F32),
+        in_specs=scalars(1) + whole(2 + parts),
+        out_specs=pl.BlockSpec(memory_space=VMEM),
+        scratch_shapes=[VMEM(kept.shape, F32)],
+    )(info, coming, kept, *transfers)
+
+
+def paired(columns, tiles, boundary, row_tensors, sketch_bond, sketch_phys, edge_factor, closing, left_edge):
+    planes, rows = columns // 2, tiles // 2
+
+    def number(z, c, y, x):
+        return (2 * z + c) * tiles + 2 * y + x
+
+    every = [(z, c, y, x) for z in range(planes) for c in range(2) for y in range(rows) for x in range(2)]
+
+    def which(z, x):
+        return x ^ (z & 1)
+
+    def fetch(i):
+        return [(number(z, which(z, x), (y + i) % rows, x ^ c), number(z, c, y, x)) for z, c, y, x in every]
+
+    home = [(b, a) for a, b in fetch(0)]
+    core = [(number(z, c, y, x), number(z, 1 - c, y, x)) for z, c, y, x in every]
+    cross = [(number(z, c, y, x), number(z, c, y, 1 - x)) for z, c, y, x in every]
+
+    def turned(i):
+        return [(number(z, c, (y + i) % rows, x), number(z, c, y, x)) for z, c, y, x in every]
+
+    def right_of(z, c, y, x):
+        if which(z, x) == 0:
+            return number(z, c, y, 1 - x)
+        return number(z + 1, c, y, x) if z + 1 < planes else None
+
+    right = [(number(*d), right_of(*d)) for d in every if right_of(*d) is not None]
+    edge_route = [(number(0, 1, y, 1), number(0, 1, y, 0)) for y in range(rows)]
+
+    def move(block, route):
+        return lax.ppermute(block, AXES, route)
+
+    col, tile = lax.axis_index("col"), lax.axis_index("tile")
+    z, c, y, x = col // 2, col % 2, tile // 2, tile % 2
+    s = (x + z) % 2
+    site_number = 2 * z + s
+    own_column = c == s
+
+    share, legs, width = boundary.shape[1:]
+    size = width // tiles
+
+    small = jnp.concatenate(
+        [
+            sketch_phys[0].reshape(legs * legs, width).astype(F32),
+            jnp.pad(
+                jnp.concatenate([row_tensors[0].reshape(-1).astype(F32), closing[0]]),
+                (0, width - legs**4 - legs),
+            )[None],
+        ]
+    )
+    small = jnp.where(own_column, small, move(small, core))
+    row_tensor = small[-1, : legs**4].reshape(legs, legs, legs, legs)
+    weights = small[-1, legs**4 : legs**4 + legs]
+    phys_map = jnp.einsum(
+        "lurd,ldk->kur",
+        row_tensor,
+        small[:-1].reshape(legs, legs, width),
+        precision=lax.Precision.HIGHEST,
+    ).reshape(width, legs * legs)
+    step = size // (legs * legs)
+    mix = jnp.einsum("lurd,ab->dlaurb", row_tensor, jnp.eye(step, dtype=F32))
+    mix = mix.reshape(legs * legs * step, legs * legs * step).astype(BF16)
+
+    ahead = jnp.arange(rows, dtype=jnp.int32)
+    near = 2 * ((y + ahead) % rows) + (x + c) % 2
+    far = 2 * ((y + ahead) % rows) + (x + c + 1) % 2
+    spots = jnp.concatenate([near, far]).astype(jnp.int32)
+
+    bonds = [move(sketch_bond[0], fetch(i)) for i in range(rows)]
+    bonds += [move(b, core) for b in bonds]
+    site = boundary[0].transpose(1, 0, 2)
+    sites = [move(site, fetch(i)) for i in range(rows)]
+
+    range_rows, panels = [], []
+    for block in sites:
+        rows_t, panels = sketch(spots, phys_map, bonds, block, panels)
+        range_rows.append(rows_t)
+    others = [move(p, core) for p in panels]
+    site_a = jnp.stack(sites)
+    site_a, _ = lax.optimization_barrier((site_a, others[0]))
+    site_b = move(site_a, core)
+
+    edge, _ = lax.optimization_barrier((edge_factor, others[0]))
+    edge = jnp.where(c == 0, edge, move(edge, edge_route))
+    edge = edge.transpose(2, 1, 0).reshape(width, legs * share)
+
+    lows, highs, rests, lefts = [], [], [], []
+    for turn in range(tiles):
+        out = basis_columns(turn, panels[turn], others[turn], lows, highs, rests, range_rows)
+        if turn < tiles - 1:
+            lows.append(out[0])
+            rests.append(out[2])
+        highs.append(out[-1] if turn == tiles - 1 else out[1])
+        come = move(highs[turn][0], right)
+        come = jnp.where(site_number == 0, edge[turn * size : (turn + 1) * size], come)
+        mine = [come] + [move(come, turned(i)) for i in range(1, rows)]
+        lefts.append(mine + [move(m, core) for m in mine])
+
+    def picked(q):
+        out = highs[0]
+        for turn in range(1, tiles):
+            out = jnp.where(q == turn, highs[turn], out)
+        return out
+
+    basis_b = move(picked(far[0]), core)
+    absorbed = absorb(mix, picked(near[0]), basis_b, site_a, site_b)
+
+    source = jnp.where(s == 1, 1 - x, x)
+    near_left = 2 * ((y + ahead) % rows) + (source + c) % 2
+    far_left = 2 * ((y + ahead) % rows) + (source + c + 1) % 2
+    left_spots = jnp.concatenate([near_left, far_left]).astype(jnp.int32)
+    new_parts, transfer_parts = [], []
+    for turn in range(tiles):
+        new, transfer = close(left_spots, weights, absorbed, lefts[turn])
+        new_parts.append(move(new, home))
+        transfer_parts.append(transfer)
+    new_site = jnp.concatenate(new_parts, axis=2).transpose(1, 0, 2)
+
+    transfer = jnp.concatenate(transfer_parts, axis=1)
+    transfers = [transfer] + [move(transfer, turned(i)) for i in range(1, rows)]
+    transfers += [move(t, core) for t in transfers]
+
+    env = left_edge[None]
+    kept = env
+    for turn in range(columns):
+        if turn:
+            route = [(a, b) for (a, b), d in zip(right, (d for d in every if right_of(*d) is not None)) if 2 * d[0] + which(d[0], d[3]) == turn - 1]
+            env = move(kept, route)
+        info = jnp.concatenate([spots, (site_number == turn).astype(jnp.int32)[None]])
+        kept = relay(info, env, kept, transfers)
+    env = jnp.where(own_column, kept, move(kept, cross))
+    env = lax.dynamic_slice_in_dim(env, tile * share, share, axis=1)
+    return new_site[None], env
+
+
 def solution(mesh):
     in_specs = (
         P("col", "tile", None, None),
@@ -87,4 +570,13 @@
         P(),
     )
     out_specs = (P("col", "tile", None, None), P("col", "tile"))
+    columns, tiles = mesh.shape["col"], mesh.shape["tile"]
+
+    def local(*args):
+        share, legs, width = args[0].shape[1:]
+        even = columns % 2 == 0 and tiles % 2 == 0
+        if even and share % (2 * LANES) == 0 and share == width // tiles and legs**4 + legs <= width:
+            return paired(columns, tiles, *args)
+        return plain(*args)
+
     return jax.shard_map(local, mesh=mesh, in_specs=in_specs, out_specs=out_specs, check_vma=False)

time: 947 us -> 410 us (0.43)
  the two profiles are of different devices: /device:TPU:8 before, /device:TPU:31 now
where the time goes in v1:
time: 410 us; the launch traced here: 404 us
  Pallas kernels  161 us (39%)
  waiting for transfers between devices  119 us (29%)
  starting transfers between devices  77.1 us (19%)
  local copies, waits for them, and re-layouts  25.6 us (6%)
  other arithmetic  18.3 us (4%)
    ppermute x45, waiting for transfers between devices, move(): return lax.ppermute(block, AXES, route)  119 us
    ppermute x45, starting transfers between devices, move(): return lax.ppermute(block, AXES, route)  77.1 us
    pallas_call x4, Pallas kernels, basis_columns(): call(functools.partial(basis_kernel, turn, groups, last), 'basis', 150000...  73.8 us
    pallas_call x2, Pallas kernels, sketch(): call(functools.partial(sketch_kernel, parts, not before), 'sketch', 50000...  33.2 us
    pallas_call x4, Pallas kernels, close(): call(functools.partial(close_kernel, parts, legs), 'close', 3000000000.0,...  27.7 us
    pallas_call x1, Pallas kernels, absorb(): call(functools.partial(absorb_kernel, legs), 'absorb', 15000000000.0, 48,...  15.4 us
    unnamed x45, local copies, waits for them, and re-layouts  13.2 us
    pallas_call x8, Pallas kernels, relay(): call(functools.partial(relay_kernel, parts), 'relay', 100000000.0, 24, ou...  10.4 us
  transfers between devices with their start and end apart: 45, of which 9 were waited for; matrix products, arithmetic and copies ran while one was open for 9% of the time, Pallas kernels for 32%

profile of v1, /device:TPU:31, one launch (start us, length us, event | category | flops | bytes accessed | tf_op | source)
XLA Modules:
  0.0 403.5 jit_solution(325340093207438957)
XLA Ops:
  0.7 3.6 copy.42
  4.3 2.2 collective-permute-start.6
  7.1 3.0 collective-permute-start.1
  11.4 13.7 %collective-permute-start = (f32[17,1024]{1,0:T(8,128)S(1)}, f32[17,1024]{1,0:T(8,128)S(1)}, u32[]{:S(2)}, u32[]{:S(2)}) collective-permute-start(f32[17,1024]{1,0:T(8,128)S(1)} %pad_maximum_fusion.1), channel_id=1, source_target_pairs={{0,4},{1,5},{2,6},{3,7},{4,0},{5,1},{6,2},{7,3},{8,12},{9,13},{10,... | collective-permute-start | bytes 208904 | tf_op jit(solution)/shard_map/ppermute | solution.py:457
  25.1 35.3 %collective-permute-done.1.refs_0_ = bf16[256,1024]{1,0:T(8,128)(2,1)S(1)} collective-permute-done((bf16[256,1024]{1,0:T(8,128)(2,1)S(1)}, bf16[256,1024]{1,0:T(8,128)(2,1)S(1)}, u32[]{:S(2)}, u32[]{:S(2)}) %collective-permute-start.1) | collective-permute-done | bytes 524320 | tf_op jit(solution)/shard_map/ppermute | solution.py:457
  60.4 5.3 %collective-permute-done.2.refs_1_ = bf16[256,1024]{1,0:T(8,128)(2,1)S(1)} collective-permute-done((bf16[256,1024]{1,0:T(8,128)(2,1)S(1)}, bf16[256,1024]{1,0:T(8,128)(2,1)S(1)}, u32[]{:S(2)}, u32[]{:S(2)}) %collective-permute-start.2) | collective-permute-done | bytes 524320 | tf_op jit(solution)/shard_map/ppermute | solution.py:457
  65.6 16.4 %collective-permute-start.4 = (bf16[256,1024]{1,0:T(8,128)(2,1)S(1)}, bf16[256,1024]{1,0:T(8,128)(2,1)S(1)}, u32[]{:S(2)}, u32[]{:S(2)}) collective-permute-start(bf16[256,1024]{1,0:T(8,128)(2,1)S(1)} %collective-permute-done.2.refs_1_), channel_id=1, source_target_pairs={{0,4},{1,5},{2,6},{3,7},{4,0},{5,1},{6,2},{7,3},{8,12},{9,13},{10,... | collective-permute-start | bytes 1572872 | tf_op jit(solution)/shard_map/ppermute | solution.py:457
  83.6 10.6 %sketch.2 = (f32[1024,1024]{1,0:T(8,128)}, f32[1024,256]{1,0:T(8,128)S(1)}, f32[768,256]{1,0:T(8,128)S(1)}, f32[512,256]{1,0:T(8,128)S(1)}, f32[256,256]{1,0:T(8,128)S(1)}) custom-call(s32[4]{0:T(128)S(1)} %pad_add_fusion.1.where_ref, f32[1024,16]{1,0:T(8,128)S(1)} %convolution_bitcast_fusion.map_ref, bf16[256,1024]{1,0:T(8,128)(2,1)S(1)} %collective-permute-done.1.refs_0_, ...), custom_call_target="tpu_custom_call" | custom-call | flops 5000000000 | bytes 1048576 | tf_op jit(solution)/shard_map/sketch/pallas_call | solution.py:222
  95.2 22.6 %sketch.3 = (f32[1024,1024]{1,0:T(8,128)}, f32[1024,256]{1,0:T(8,128)}, f32[768,256]{1,0:T(8,128)S(1)}, f32[512,256]{1,0:T(8,128)S(1)}, f32[256,256]{1,0:T(8,128)S(1)}) custom-call(s32[4]{0:T(128)S(1)} %pad_add_fusion.1.where_ref, f32[1024,16]{1,0:T(8,128)S(1)} %convolution_bitcast_fusion.map_ref, bf16[256,1024]{1,0:T(8,128)(2,1)S(1)} %collective-permute-done.1.refs_0_, ...), custom_call_target="tpu_custom_call" | custom-call | flops 5000000000 | bytes 1048576 | tf_op jit(solution)/shard_map/sketch/pallas_call | solution.py:222
  119.9 4.7 %pad_maximum_fusion.site_a = bf16[2,4,256,1024]{3,2,1,0:T(8,128)(2,1)} fusion(bf16[1,4,256,1024]{3,2,1,0:T(8,128)(2,1)} %bitcast.19, bf16[1,4,256,1024]{3,2,1,0:T(8,128)(2,1)} %bitcast.18), kind=kLoop, calls=%fused_computation | loop fusion | flops 2097152 | bytes 8388608 | tf_op jit(solution)/shard_map/stack | solution.py:505
  124.9 2.0 collective-permute-start.13
  126.9 15.5 %basis.4 = (f32[768,256]{1,0:T(8,128)}, bf16[2,256,1024]{2,1,0:T(8,128)(2,1)}, bf16[2,256,1024]{2,1,0:T(8,128)(2,1)}) custom-call(f32[1024,256]{1,0:T(8,128)} %get-tuple-element.36.refs_0_, f32[1024,256]{1,0:T(8,128)} %collective-permute-done.8.refs_1_, f32[1024,1024]{1,0:T(8,128)} %get-tuple-element.37.refs_2_.refs_5_.refs_8_.refs_11_, ...), custom_call_target="tpu_custom_call" | custom-call | flops 15000000512 | bytes 1048576 | tf_op jit(solution)/shard_map/basis/pallas_call | solution.py:284
  143.3 18.5 %basis.5 = (f32[512,256]{1,0:T(8,128)}, bf16[2,256,1024]{2,1,0:T(8,128)(2,1)}, bf16[2,256,1024]{2,1,0:T(8,128)(2,1)}) custom-call(f32[768,256]{1,0:T(8,128)} %copy-done.1, f32[768,256]{1,0:T(8,128)} %copy-done.14, f32[768,256]{1,0:T(8,128)} %get-tuple-element.39.refs_2_, bf16[2,256,1024]{2,1,0:T(8,128)(2,1)} %get-tuple-element.41.refs_3_.refs_4_.refs_5_, ...), custom_call_target="tpu_custom_call" | custom-call | flops 15000000512 | bytes 1048576 | tf_op jit(solution)/shard_map/basis/pallas_call | solution.py:284
  162.7 19.8 %basis.6 = (f32[256,256]{1,0:T(8,128)}, bf16[2,256,1024]{2,1,0:T(8,128)(2,1)}, bf16[2,256,1024]{2,1,0:T(8,128)(2,1)}) custom-call(f32[512,256]{1,0:T(8,128)} %copy-done.2, f32[512,256]{1,0:T(8,128)} %copy-done.16, f32[768,256]{1,0:T(8,128)} %get-tuple-element.39.refs_2_, f32[512,256]{1,0:T(8,128)} %get-tuple-element.43.refs_3_, ...), custom_call_target="tpu_custom_call" | custom-call | flops 15000000512 | bytes 1048576 | tf_op jit(solution)/shard_map/basis/pallas_call | solution.py:284
  183.1 20.0 %basis.7 = bf16[2,256,1024]{2,1,0:T(8,128)(2,1)} custom-call(f32[256,256]{1,0:T(8,128)} %copy-done.5, f32[256,256]{1,0:T(8,128)} %copy-done.17, f32[768,256]{1,0:T(8,128)} %get-tuple-element.39.refs_2_, f32[512,256]{1,0:T(8,128)} %get-tuple-element.43.refs_3_, f32[256,256]{1,0:T(8,128)} %get-tuple-element.47.refs_4_, ...), custom_call_target="tpu_custom_call" | custom-call | flops 15000000512 | bytes 1048576 | tf_op jit(solution)/shard_map/basis/pallas_call | solution.py:284
  203.2 2.5 select_select_fusion
  206.8 1.9 collective-permute-start.29
  209.5 1.9 collective-permute-start.24
  213.1 1.9 collective-permute-start.19
  215.0 2.7 select_bitcast_fusion
  217.7 1.5 fusion.5
  220.7 12.7 %collective-permute-done.24 = bf16[256,1024]{1,0:T(8,128)(2,1)} collective-permute-done((bf16[256,1024]{1,0:T(8,128)(2,1)}, bf16[256,1024]{1,0:T(8,128)(2,1)}, u32[]{:S(2)}, u32[]{:S(2)}) %collective-permute-start.24) | collective-permute-done | bytes 524320 | tf_op jit(solution)/shard_map/ppermute | solution.py:457
  233.5 2.6 collective-permute-start.14
  237.2 7.5 %collective-permute-done.19 = bf16[256,1024]{1,0:T(8,128)(2,1)} collective-permute-done((bf16[256,1024]{1,0:T(8,128)(2,1)}, bf16[256,1024]{1,0:T(8,128)(2,1)}, u32[]{:S(2)}, u32[]{:S(2)}) %collective-permute-start.19) | collective-permute-done | bytes 524320 | tf_op jit(solution)/shard_map/ppermute | solution.py:457
  246.8 9.2 %collective-permute-done.14 = bf16[256,1024]{1,0:T(8,128)(2,1)} collective-permute-done((bf16[256,1024]{1,0:T(8,128)(2,1)}, bf16[256,1024]{1,0:T(8,128)(2,1)}, u32[]{:S(2)}, u32[]{:S(2)}) %collective-permute-start.14) | collective-permute-done | bytes 524320 | tf_op jit(solution)/shard_map/ppermute | solution.py:457
  257.3 1.3 collective-permute-start.15
  258.6 1.4 fusion
  260.0 2.9 convert_element_type.36.mix_ref
  262.9 2.2 copy.28
  267.3 1.7 collective-permute-start.21
  269.4 10.3 %collective-permute-done.15.refs_1_ = bf16[256,1024]{1,0:T(8,128)(2,1)} collective-permute-done((bf16[256,1024]{1,0:T(8,128)(2,1)S(1)}, bf16[256,1024]{1,0:T(8,128)(2,1)}, u32[]{:S(2)}, u32[]{:S(2)}) %collective-permute-start.15) | collective-permute-done | bytes 524320 | tf_op jit(solution)/shard_map/ppermute | solution.py:457
  279.6 3.6 collective-permute-start.22
  283.2 15.4 %absorb.1.absorbed = bf16[4,1024,1024]{2,1,0:T(8,128)(2,1)} custom-call(bf16[256,256]{1,0:T(8,128)(2,1)S(1)} %convert_element_type.36.mix_ref, bf16[2,256,1024]{2,1,0:T(8,128)(2,1)S(1)} %get-tuple-element.67.basis_a, bf16[2,256,1024]{2,1,0:T(8,128)(2,1)} %collective-permute-done.11.basis_b, bf16[2,4,256,1024]{3,2,1,0:T(8,128)(2,1)} %pad_maximum_fusion.site_a, ...), custom_call_target="tpu_custom_call" | custom-call | flops 15000000512 | bytes 1048576 | tf_op jit(solution)/shard_map/absorb/pallas_call | solution.py:327
  300.4 6.3 %close.5 = (bf16[4,256,256]{2,1,0:T(8,128)(2,1)S(1)}, bf16[256,256]{1,0:T(8,128)(2,1)S(1)}) custom-call(s32[4]{0:T(128)S(1)} %pad_add_fusion.where_ref, f32[4]{0:T(128)S(1)} %slice_bitcast_fusion.4.weights, bf16[4,1024,1024]{2,1,0:T(8,128)(2,1)} %absorb.1.absorbed, bf16[256,1024]{1,0:T(8,128)(2,1)S(1)} %broadcast_select_fusion.2.refs_0_, ...), custom_call_target="tpu_custom_call" | custom-call | flops 3000000000 | bytes 1048576 | tf_op jit(solution)/shard_map/close/pallas_call | solution.py:370
  307.2 7.1 %close.4 = (bf16[4,256,256]{2,1,0:T(8,128)(2,1)}, bf16[256,256]{1,0:T(8,128)(2,1)S(1)}) custom-call(s32[4]{0:T(128)S(1)} %pad_add_fusion.where_ref, f32[4]{0:T(128)S(1)} %slice_bitcast_fusion.4.weights, bf16[4,1024,1024]{2,1,0:T(8,128)(2,1)} %absorb.1.absorbed, bf16[256,1024]{1,0:T(8,128)(2,1)S(1)} %broadcast_select_fusion.3.refs_0_, ...), custom_call_target="tpu_custom_call" | custom-call | flops 3000000000 | bytes 1048576 | tf_op jit(solution)/shard_map/close/pallas_call | solution.py:370
  314.4 7.3 %close.6 = (bf16[4,256,256]{2,1,0:T(8,128)(2,1)}, bf16[256,256]{1,0:T(8,128)(2,1)S(1)}) custom-call(s32[4]{0:T(128)S(1)} %pad_add_fusion.where_ref, f32[4]{0:T(128)S(1)} %slice_bitcast_fusion.4.weights, bf16[4,1024,1024]{2,1,0:T(8,128)(2,1)} %absorb.1.absorbed, bf16[256,1024]{1,0:T(8,128)(2,1)S(1)} %broadcast_select_fusion.1.refs_0_, ...), custom_call_target="tpu_custom_call" | custom-call | flops 3000000000 | bytes 1048576 | tf_op jit(solution)/shard_map/close/pallas_call | solution.py:370
  321.8 7.0 %close.7 = (bf16[4,256,256]{2,1,0:T(8,128)(2,1)}, bf16[256,256]{1,0:T(8,128)(2,1)S(1)}) custom-call(s32[4]{0:T(128)S(1)} %pad_add_fusion.where_ref, f32[4]{0:T(128)S(1)} %slice_bitcast_fusion.4.weights, bf16[4,1024,1024]{2,1,0:T(8,128)(2,1)} %absorb.1.absorbed, bf16[256,1024]{1,0:T(8,128)(2,1)S(1)} %broadcast_select_fusion.refs_0_, ...), custom_call_target="tpu_custom_call" | custom-call | flops 3000000000 | bytes 1048576 | tf_op jit(solution)/shard_map/close/pallas_call | solution.py:370
  329.8 12.2 %collective-permute-done.34.refs_1_ = bf16[256,1024]{1,0:T(8,128)(2,1)S(1)} collective-permute-done((bf16[256,1024]{1,0:T(8,128)(2,1)S(1)}, bf16[256,1024]{1,0:T(8,128)(2,1)S(1)}, u32[]{:S(2)}, u32[]{:S(2)}) %collective-permute-start.34) | collective-permute-done | bytes 524320 | tf_op jit(solution)/shard_map/ppermute | solution.py:457
  343.2 1.9 collective-permute-start.33
  345.1 2.3 collective-permute-start.28
  347.4 3.4 collective-permute-start.23
  350.8 1.9 collective-permute-start.18
  352.9 1.3 relay.8.kept
  354.9 1.3 relay.9.kept
  365.5 26.2 %collective-permute-done.42.coming = f32[1,1024]{1,0:T(1,128)S(1)} collective-permute-done((f32[1,1024]{1,0:T(1,128)S(1)}, f32[1,1024]{1,0:T(1,128)S(1)}, u32[]{:S(2)}, u32[]{:S(2)}) %collective-permute-start.42) | collective-permute-done | bytes 4128 | tf_op jit(solution)/shard_map/ppermute | solution.py:457
  396.3 1.9 collective-permute-start.44
  398.2 1.6 maximum_bitcast_fusion
  399.8 2.9 copy.29
  (147 shorter events, 41.0 us)
Async XLA Ops:
  4.3 79.4 %collective-permute-start.6 = (bf16[4,256,1024]{2,1,0:T(8,128)(2,1)}, bf16[4,256,1024]{2,1,0:T(8,128)(2,1)}, u32[]{:S(2)}, u32[]{:S(2)}) collective-permute-start(bf16[4,256,1024]{2,1,0:T(8,128)(2,1)} %bitcast.58), channel_id=1, source_target_pairs={{0,0},{5,1},{2,2},{7,3},{1,4},{4,5},{3,6},{6,7},{12,8},{9,9},{14,1... | collective-permute-start | bytes 6291464 | tf_op jit(solution)/shard_map/ppermute | solution.py:457
  6.4 88.8 %collective-permute-start.5 = (bf16[4,256,1024]{2,1,0:T(8,128)(2,1)}, bf16[4,256,1024]{2,1,0:T(8,128)(2,1)}, u32[]{:S(2)}, u32[]{:S(2)}) collective-permute-start(bf16[4,256,1024]{2,1,0:T(8,128)(2,1)} %bitcast.58), channel_id=1, source_target_pairs={{2,0},{7,1},{0,2},{5,3},{3,4},{6,5},{1,6},{4,7},{14,8},{11,9},{12,... | collective-permute-start | bytes 6291464 | tf_op jit(solution)/shard_map/ppermute | solution.py:457
  7.1 53.2 %collective-permute-start.1 = (bf16[256,1024]{1,0:T(8,128)(2,1)S(1)}, bf16[256,1024]{1,0:T(8,128)(2,1)S(1)}, u32[]{:S(2)}, u32[]{:S(2)}) collective-permute-start(bf16[256,1024]{1,0:T(8,128)(2,1)S(1)} %bitcast.81), channel_id=1, source_target_pairs={{0,0},{5,1},{2,2},{7,3},{1,4},{4,5},{3,6},{6,7},{12,8},{9,9},{14,1... | collective-permute-start | bytes 1572872 | tf_op jit(solution)/shard_map/ppermute | solution.py:457
  10.1 55.5 %collective-permute-start.2 = (bf16[256,1024]{1,0:T(8,128)(2,1)S(1)}, bf16[256,1024]{1,0:T(8,128)(2,1)S(1)}, u32[]{:S(2)}, u32[]{:S(2)}) collective-permute-start(bf16[256,1024]{1,0:T(8,128)(2,1)S(1)} %bitcast.82), channel_id=1, source_target_pairs={{2,0},{7,1},{0,2},{5,3},{3,4},{6,5},{1,6},{4,7},{14,8},{11,9},{12,... | collective-permute-start | bytes 1572872 | tf_op jit(solution)/shard_map/ppermute | solution.py:457
  11.4 70.7 %collective-permute-start = (f32[17,1024]{1,0:T(8,128)S(1)}, f32[17,1024]{1,0:T(8,128)S(1)}, u32[]{:S(2)}, u32[]{:S(2)}) collective-permute-start(f32[17,1024]{1,0:T(8,128)S(1)} %pad_maximum_fusion.1), channel_id=1, source_target_pairs={{0,4},{1,5},{2,6},{3,7},{4,0},{5,1},{6,2},{7,3},{8,12},{9,13},{10,... | collective-permute-start | bytes 208904 | tf_op jit(solution)/shard_map/ppermute | solution.py:457
  60.4 23.2 %collective-permute-start.3 = (bf16[256,1024]{1,0:T(8,128)(2,1)S(1)}, bf16[256,1024]{1,0:T(8,128)(2,1)S(1)}, u32[]{:S(2)}, u32[]{:S(2)}) collective-permute-start(bf16[256,1024]{1,0:T(8,128)(2,1)S(1)} %collective-permute-done.1.refs_0_), channel_id=1, source_target_pairs={{0,4},{1,5},{2,6},{3,7},{4,0},{5,1},{6,2},{7,3},{8,12},{9,13},{10,... | collective-permute-start | bytes 1572872 | tf_op jit(solution)/shard_map/ppermute | solution.py:457
  65.6 18.0 %collective-permute-start.4 = (bf16[256,1024]{1,0:T(8,128)(2,1)S(1)}, bf16[256,1024]{1,0:T(8,128)(2,1)S(1)}, u32[]{:S(2)}, u32[]{:S(2)}) collective-permute-start(bf16[256,1024]{1,0:T(8,128)(2,1)S(1)} %collective-permute-done.2.refs_1_), channel_id=1, source_target_pairs={{0,4},{1,5},{2,6},{3,7},{4,0},{5,1},{6,2},{7,3},{8,12},{9,13},{10,... | collective-permute-start | bytes 1572872 | tf_op jit(solution)/shard_map/ppermute | solution.py:457
  118.5 6.1 %collective-permute-start.8 = (f32[1024,256]{1,0:T(8,128)}, f32[1024,256]{1,0:T(8,128)}, u32[]{:S(2)}, u32[]{:S(2)}) collective-permute-start(f32[1024,256]{1,0:T(8,128)} %get-tuple-element.36.refs_0_), channel_id=1, source_target_pairs={{0,4},{1,5},{2,6},{3,7},{4,0},{5,1},{6,2},{7,3},{8,12},{9,13},{10,... | collective-permute-start | bytes 3145736 | tf_op jit(solution)/shard_map/ppermute | solution.py:457
  119.1 63.3 %collective-permute-start.7 = (f32[256,256]{1,0:T(8,128)}, f32[256,256]{1,0:T(8,128)S(1)}, u32[]{:S(2)}, u32[]{:S(2)}) collective-permute-start(f32[256,256]{1,0:T(8,128)} %copy-done.5), channel_id=1, source_target_pairs={{0,4},{1,5},{2,6},{3,7},{4,0},{5,1},{6,2},{7,3},{8,12},{9,13},{10,... | collective-permute-start | bytes 786440 | tf_op jit(solution)/shard_map/ppermute | solution.py:457
  119.4 23.0 %collective-permute-start.9 = (f32[768,256]{1,0:T(8,128)S(1)}, f32[768,256]{1,0:T(8,128)S(1)}, u32[]{:S(2)}, u32[]{:S(2)}) collective-permute-start(f32[768,256]{1,0:T(8,128)S(1)} %get-tuple-element.40.refs_0_), channel_id=1, source_target_pairs={{0,4},{1,5},{2,6},{3,7},{4,0},{5,1},{6,2},{7,3},{8,12},{9,13},{10,... | collective-permute-start | bytes 2359304 | tf_op jit(solution)/shard_map/ppermute | solution.py:457
  119.6 42.2 %collective-permute-start.10 = (f32[512,256]{1,0:T(8,128)S(1)}, f32[512,256]{1,0:T(8,128)S(1)}, u32[]{:S(2)}, u32[]{:S(2)}) collective-permute-start(f32[512,256]{1,0:T(8,128)S(1)} %get-tuple-element.44.refs_0_), channel_id=1, source_target_pairs={{0,4},{1,5},{2,6},{3,7},{4,0},{5,1},{6,2},{7,3},{8,12},{9,13},{10,... | collective-permute-start | bytes 1572872 | tf_op jit(solution)/shard_map/ppermute | solution.py:457
  124.6 158.7 %collective-permute-start.12 = (bf16[2,4,256,1024]{3,2,1,0:T(8,128)(2,1)}, bf16[2,4,256,1024]{3,2,1,0:T(8,128)(2,1)}, u32[]{:S(2)}, u32[]{:S(2)}) collective-permute-start(bf16[2,4,256,1024]{3,2,1,0:T(8,128)(2,1)} %pad_maximum_fusion.site_a), channel_id=1, source_target_pairs={{0,4},{1,5},{2,6},{3,7},{4,0},{5,1},{6,2},{7,3},{8,12},{9,13},{10,... | collective-permute-start | bytes 12582920 | tf_op jit(solution)/shard_map/ppermute | solution.py:457
  124.9 88.2 %collective-permute-start.13 = (bf16[256,4,1024]{2,1,0:T(4,128)(2,1)}, bf16[256,4,1024]{2,1,0:T(4,128)(2,1)}, u32[]{:S(2)}, u32[]{:S(2)}) collective-permute-start(bf16[256,4,1024]{2,1,0:T(4,128)(2,1)} %param.11), channel_id=1, source_target_pairs={{5,4},{7,6}} | collective-permute-start | bytes 6291464 | tf_op jit(solution)/shard_map/ppermute | solution.py:457
  183.1 20.0 %copy-start.9 = (bf16[2,256,1024]{2,1,0:T(8,128)(2,1)S(1)}, bf16[2,256,1024]{2,1,0:T(8,128)(2,1)}, u32[]{:S(2)}) copy-start(bf16[2,256,1024]{2,1,0:T(8,128)(2,1)} %get-tuple-element.48.refs_7_) | copy-start | bytes 3145732
  205.7 61.6 %collective-permute-start.11 = (bf16[2,256,1024]{2,1,0:T(8,128)(2,1)}, bf16[2,256,1024]{2,1,0:T(8,128)(2,1)}, u32[]{:S(2)}, u32[]{:S(2)}) collective-permute-start(bf16[2,256,1024]{2,1,0:T(8,128)(2,1)} %get-tuple-element.66), channel_id=1, source_target_pairs={{0,4},{1,5},{2,6},{3,7},{4,0},{5,1},{6,2},{7,3},{8,12},{9,13},{10,... | collective-permute-start | bytes 3145736 | tf_op jit(solution)/shard_map/ppermute | solution.py:457
  206.8 50.5 %collective-permute-start.29 = (bf16[256,1024]{1,0:T(8,128)(2,1)}, bf16[256,1024]{1,0:T(8,128)(2,1)}, u32[]{:S(2)}, u32[]{:S(2)}) collective-permute-start(bf16[256,1024]{1,0:T(8,128)(2,1)} %slice_bitcast_fusion), channel_id=1, source_target_pairs={{0,1},{1,9},{2,3},{3,11},{4,5},{5,13},{6,7},{7,15},{8,16},{9,8},{1... | collective-permute-start | bytes 1572872 | tf_op jit(solution)/shard_map/ppermute | solution.py:457
  209.5 23.9 %collective-permute-start.24 = (bf16[256,1024]{1,0:T(8,128)(2,1)}, bf16[256,1024]{1,0:T(8,128)(2,1)}, u32[]{:S(2)}, u32[]{:S(2)}) collective-permute-start(bf16[256,1024]{1,0:T(8,128)(2,1)} %slice_bitcast_fusion.1), channel_id=1, source_target_pairs={{0,1},{1,9},{2,3},{3,11},{4,5},{5,13},{6,7},{7,15},{8,16},{9,8},{1... | collective-permute-start | bytes 1572872 | tf_op jit(solution)/shard_map/ppermute | solution.py:457
  213.1 31.6 %collective-permute-start.19 = (bf16[256,1024]{1,0:T(8,128)(2,1)}, bf16[256,1024]{1,0:T(8,128)(2,1)}, u32[]{:S(2)}, u32[]{:S(2)}) collective-permute-start(bf16[256,1024]{1,0:T(8,128)(2,1)} %slice_bitcast_fusion.2), channel_id=1, source_target_pairs={{0,1},{1,9},{2,3},{3,11},{4,5},{5,13},{6,7},{7,15},{8,16},{9,8},{1... | collective-permute-start | bytes 1572872 | tf_op jit(solution)/shard_map/ppermute | solution.py:457
  233.5 22.5 %collective-permute-start.14 = (bf16[256,1024]{1,0:T(8,128)(2,1)}, bf16[256,1024]{1,0:T(8,128)(2,1)}, u32[]{:S(2)}, u32[]{:S(2)}) collective-permute-start(bf16[256,1024]{1,0:T(8,128)(2,1)} %slice_bitcast_fusion.3), channel_id=1, source_target_pairs={{0,1},{1,9},{2,3},{3,11},{4,5},{5,13},{6,7},{7,15},{8,16},{9,8},{1... | collective-permute-start | bytes 1572872 | tf_op jit(solution)/shard_map/ppermute | solution.py:457
  244.7 24.3 %collective-permute-start.25 = (bf16[256,1024]{1,0:T(8,128)(2,1)S(1)}, bf16[256,1024]{1,0:T(8,128)(2,1)}, u32[]{:S(2)}, u32[]{:S(2)}) collective-permute-start(bf16[256,1024]{1,0:T(8,128)(2,1)S(1)} %broadcast_select_fusion.1.refs_0_), channel_id=1, source_target_pairs={{2,0},{3,1},{0,2},{1,3},{6,4},{7,5},{4,6},{5,7},{10,8},{11,9},{8,1... | collective-permute-start | bytes 1572872 | tf_op jit(solution)/shard_map/ppermute | solution.py:457
  255.9 13.2 %collective-permute-start.20 = (bf16[256,1024]{1,0:T(8,128)(2,1)S(1)}, bf16[256,1024]{1,0:T(8,128)(2,1)S(1)}, u32[]{:S(2)}, u32[]{:S(2)}) collective-permute-start(bf16[256,1024]{1,0:T(8,128)(2,1)S(1)} %broadcast_select_fusion.2.refs_0_), channel_id=1, source_target_pairs={{2,0},{3,1},{0,2},{1,3},{6,4},{7,5},{4,6},{5,7},{10,8},{11,9},{8,1... | collective-permute-start | bytes 1572872 | tf_op jit(solution)/shard_map/ppermute | solution.py:457
  257.3 22.3 %collective-permute-start.15 = (bf16[256,1024]{1,0:T(8,128)(2,1)S(1)}, bf16[256,1024]{1,0:T(8,128)(2,1)}, u32[]{:S(2)}, u32[]{:S(2)}) collective-permute-start(bf16[256,1024]{1,0:T(8,128)(2,1)S(1)} %broadcast_select_fusion.3.refs_0_), channel_id=1, source_target_pairs={{2,0},{3,1},{0,2},{1,3},{6,4},{7,5},{4,6},{5,7},{10,8},{11,9},{8,1... | collective-permute-start | bytes 1572872 | tf_op jit(solution)/shard_map/ppermute | solution.py:457
  267.3 31.4 %collective-permute-start.21 = (bf16[256,1024]{1,0:T(8,128)(2,1)S(1)}, bf16[256,1024]{1,0:T(8,128)(2,1)S(1)}, u32[]{:S(2)}, u32[]{:S(2)}) collective-permute-start(bf16[256,1024]{1,0:T(8,128)(2,1)S(1)} %broadcast_select_fusion.2.refs_0_), channel_id=1, source_target_pairs={{0,4},{1,5},{2,6},{3,7},{4,0},{5,1},{6,2},{7,3},{8,12},{9,13},{10,... | collective-permute-start | bytes 1572872 | tf_op jit(solution)/shard_map/ppermute | solution.py:457
  269.1 38.1 %collective-permute-start.16 = (bf16[256,1024]{1,0:T(8,128)(2,1)S(1)}, bf16[256,1024]{1,0:T(8,128)(2,1)S(1)}, u32[]{:S(2)}, u32[]{:S(2)}) collective-permute-start(bf16[256,1024]{1,0:T(8,128)(2,1)S(1)} %broadcast_select_fusion.3.refs_0_), channel_id=1, source_target_pairs={{0,4},{1,5},{2,6},{3,7},{4,0},{5,1},{6,2},{7,3},{8,12},{9,13},{10,... | collective-permute-start | bytes 1572872 | tf_op jit(solution)/shard_map/ppermute | solution.py:457
  269.1 29.5 %copy-start.3 = (bf16[256,1024]{1,0:T(8,128)(2,1)}, bf16[256,1024]{1,0:T(8,128)(2,1)S(1)}, u32[]{:S(2)}) copy-start(bf16[256,1024]{1,0:T(8,128)(2,1)S(1)} %collective-permute-done.20.refs_1_) | copy-start | bytes 1572868
  269.1 37.5 %collective-permute-start.30 = (bf16[256,1024]{1,0:T(8,128)(2,1)S(1)}, bf16[256,1024]{1,0:T(8,128)(2,1)S(1)}, u32[]{:S(2)}, u32[]{:S(2)}) collective-permute-start(bf16[256,1024]{1,0:T(8,128)(2,1)S(1)} %broadcast_select_fusion.refs_0_), channel_id=1, source_target_pairs={{2,0},{3,1},{0,2},{1,3},{6,4},{7,5},{4,6},{5,7},{10,8},{11,9},{8,1... | collective-permute-start | bytes 1572872 | tf_op jit(solution)/shard_map/ppermute | solution.py:457
  279.6 19.6 %collective-permute-start.22 = (bf16[256,1024]{1,0:T(8,128)(2,1)S(1)}, bf16[256,1024]{1,0:T(8,128)(2,1)S(1)}, u32[]{:S(2)}, u32[]{:S(2)}) collective-permute-start(bf16[256,1024]{1,0:T(8,128)(2,1)S(1)} %collective-permute-done.20.refs_1_), channel_id=1, source_target_pairs={{0,4},{1,5},{2,6},{3,7},{4,0},{5,1},{6,2},{7,3},{8,12},{9,13},{10,... | collective-permute-start | bytes 1572872 | tf_op jit(solution)/shard_map/ppermute | solution.py:457
  283.2 24.0 %collective-permute-start.17 = (bf16[256,1024]{1,0:T(8,128)(2,1)}, bf16[256,1024]{1,0:T(8,128)(2,1)S(1)}, u32[]{:S(2)}, u32[]{:S(2)}) collective-permute-start(bf16[256,1024]{1,0:T(8,128)(2,1)} %collective-permute-done.15.refs_1_), channel_id=1, source_target_pairs={{0,4},{1,5},{2,6},{3,7},{4,0},{5,1},{6,2},{7,3},{8,12},{9,13},{10,... | collective-permute-start | bytes 1572872 | tf_op jit(solution)/shard_map/ppermute | solution.py:457
  298.7 15.7 %collective-permute-start.26 = (bf16[256,1024]{1,0:T(8,128)(2,1)S(1)}, bf16[256,1024]{1,0:T(8,128)(2,1)S(1)}, u32[]{:S(2)}, u32[]{:S(2)}) collective-permute-start(bf16[256,1024]{1,0:T(8,128)(2,1)S(1)} %broadcast_select_fusion.1.refs_0_), channel_id=1, source_target_pairs={{0,4},{1,5},{2,6},{3,7},{4,0},{5,1},{6,2},{7,3},{8,12},{9,13},{10,... | collective-permute-start | bytes 1572872 | tf_op jit(solution)/shard_map/ppermute | solution.py:457
  299.2 15.2 %collective-permute-start.27 = (bf16[256,1024]{1,0:T(8,128)(2,1)}, bf16[256,1024]{1,0:T(8,128)(2,1)S(1)}, u32[]{:S(2)}, u32[]{:S(2)}) collective-permute-start(bf16[256,1024]{1,0:T(8,128)(2,1)} %collective-permute-done.25.refs_1_), channel_id=1, source_target_pairs={{0,4},{1,5},{2,6},{3,7},{4,0},{5,1},{6,2},{7,3},{8,12},{9,13},{10,... | collective-permute-start | bytes 1572872 | tf_op jit(solution)/shard_map/ppermute | solution.py:457
  306.6 15.1 %collective-permute-start.31 = (bf16[256,1024]{1,0:T(8,128)(2,1)S(1)}, bf16[256,1024]{1,0:T(8,128)(2,1)S(1)}, u32[]{:S(2)}, u32[]{:S(2)}) collective-permute-start(bf16[256,1024]{1,0:T(8,128)(2,1)S(1)} %broadcast_select_fusion.refs_0_), channel_id=1, source_target_pairs={{0,4},{1,5},{2,6},{3,7},{4,0},{5,1},{6,2},{7,3},{8,12},{9,13},{10,... | collective-permute-start | bytes 1572872 | tf_op jit(solution)/shard_map/ppermute | solution.py:457
  307.1 14.6 %collective-permute-start.32 = (bf16[256,1024]{1,0:T(8,128)(2,1)S(1)}, bf16[256,1024]{1,0:T(8,128)(2,1)S(1)}, u32[]{:S(2)}, u32[]{:S(2)}) collective-permute-start(bf16[256,1024]{1,0:T(8,128)(2,1)S(1)} %collective-permute-done.30.refs_1_), channel_id=1, source_target_pairs={{0,4},{1,5},{2,6},{3,7},{4,0},{5,1},{6,2},{7,3},{8,12},{9,13},{10,... | collective-permute-start | bytes 1572872 | tf_op jit(solution)/shard_map/ppermute | solution.py:457
  321.7 31.1 %copy-start = (f32[1024]{0:T(1024)S(1)}, f32[1024]{0:T(1024)}, u32[]{:S(2)}) copy-start(f32[1024]{0:T(1024)} %param.13) | copy-start | bytes 12292
  328.8 13.1 %collective-permute-start.34 = (bf16[256,1024]{1,0:T(8,128)(2,1)S(1)}, bf16[256,1024]{1,0:T(8,128)(2,1)S(1)}, u32[]{:S(2)}, u32[]{:S(2)}) collective-permute-start(bf16[256,1024]{1,0:T(8,128)(2,1)S(1)} %constant_dynamic-update-slice_fusion.refs_0_), channel_id=1, source_target_pairs={{2,0},{3,1},{0,2},{1,3},{6,4},{7,5},{4,6},{5,7},{10,8},{11,9},{8,1... | collective-permute-start | bytes 1572872 | tf_op jit(solution)/shard_map/ppermute | solution.py:457
  329.1 21.7 %collective-permute-start.35 = (bf16[256,1024]{1,0:T(8,128)(2,1)S(1)}, bf16[256,1024]{1,0:T(8,128)(2,1)S(1)}, u32[]{:S(2)}, u32[]{:S(2)}) collective-permute-start(bf16[256,1024]{1,0:T(8,128)(2,1)S(1)} %constant_dynamic-update-slice_fusion.refs_0_), channel_id=1, source_target_pairs={{0,4},{1,5},{2,6},{3,7},{4,0},{5,1},{6,2},{7,3},{8,12},{9,13},{10,... | collective-permute-start | bytes 1572872 | tf_op jit(solution)/shard_map/ppermute | solution.py:457
  342.0 10.9 %collective-permute-start.36 = (bf16[256,1024]{1,0:T(8,128)(2,1)S(1)}, bf16[256,1024]{1,0:T(8,128)(2,1)S(1)}, u32[]{:S(2)}, u32[]{:S(2)}) collective-permute-start(bf16[256,1024]{1,0:T(8,128)(2,1)S(1)} %collective-permute-done.34.refs_1_), channel_id=1, source_target_pairs={{0,4},{1,5},{2,6},{3,7},{4,0},{5,1},{6,2},{7,3},{8,12},{9,13},{10,... | collective-permute-start | bytes 1572872 | tf_op jit(solution)/shard_map/ppermute | solution.py:457
  343.2 55.0 %collective-permute-start.33 = (bf16[4,256,256]{2,1,0:T(8,128)(2,1)}, bf16[4,256,256]{2,1,0:T(8,128)(2,1)S(1)}, u32[]{:S(2)}, u32[]{:S(2)}) collective-permute-start(bf16[4,256,256]{2,1,0:T(8,128)(2,1)} %get-tuple-element.55), channel_id=1, source_target_pairs={{0,0},{1,5},{2,2},{3,7},{4,1},{5,4},{6,3},{7,6},{8,12},{9,9},{10,1... | collective-permute-start | bytes 1572872 | tf_op jit(solution)/shard_map/ppermute | solution.py:457
  345.1 53.1 %collective-permute-start.28 = (bf16[4,256,256]{2,1,0:T(8,128)(2,1)}, bf16[4,256,256]{2,1,0:T(8,128)(2,1)}, u32[]{:S(2)}, u32[]{:S(2)}) collective-permute-start(bf16[4,256,256]{2,1,0:T(8,128)(2,1)} %get-tuple-element.54), channel_id=1, source_target_pairs={{0,0},{1,5},{2,2},{3,7},{4,1},{5,4},{6,3},{7,6},{8,12},{9,9},{10,1... | collective-permute-start | bytes 1572872 | tf_op jit(solution)/shard_map/ppermute | solution.py:457
  347.4 50.8 %collective-permute-start.23 = (bf16[4,256,256]{2,1,0:T(8,128)(2,1)S(1)}, bf16[4,256,256]{2,1,0:T(8,128)(2,1)}, u32[]{:S(2)}, u32[]{:S(2)}) collective-permute-start(bf16[4,256,256]{2,1,0:T(8,128)(2,1)S(1)} %get-tuple-element.53), channel_id=1, source_target_pairs={{0,0},{1,5},{2,2},{3,7},{4,1},{5,4},{6,3},{7,6},{8,12},{9,9},{10,1... | collective-permute-start | bytes 1572872 | tf_op jit(solution)/shard_map/ppermute | solution.py:457
  350.8 47.4 %collective-permute-start.18 = (bf16[4,256,256]{2,1,0:T(8,128)(2,1)}, bf16[4,256,256]{2,1,0:T(8,128)(2,1)}, u32[]{:S(2)}, u32[]{:S(2)}) collective-permute-start(bf16[4,256,256]{2,1,0:T(8,128)(2,1)} %get-tuple-element.52), channel_id=1, source_target_pairs={{0,0},{1,5},{2,2},{3,7},{4,1},{5,4},{6,3},{7,6},{8,12},{9,9},{10,1... | collective-permute-start | bytes 1572872 | tf_op jit(solution)/shard_map/ppermute | solution.py:457
  354.2 0.8 collective-permute-start.37
  356.2 0.7 collective-permute-start.38
  358.2 0.7 collective-permute-start.39
  360.2 0.7 collective-permute-start.40
  362.2 0.7 collective-permute-start.41
  364.2 27.5 %collective-permute-start.42 = (f32[1,1024]{1,0:T(1,128)S(1)}, f32[1,1024]{1,0:T(1,128)S(1)}, u32[]{:S(2)}, u32[]{:S(2)}) collective-permute-start(f32[1,1024]{1,0:T(1,128)S(1)} %relay.13.kept), channel_id=1, source_target_pairs={{17,25},{19,27},{21,29},{23,31}} | collective-permute-start | bytes 12296 | tf_op jit(solution)/shard_map/ppermute | solution.py:457
  393.0 2.0 collective-permute-start.43
  396.3 6.5 %collective-permute-start.44 = (f32[1,1024]{1,0:T(1,128)S(1)}, f32[1,1024]{1,0:T(1,128)S(1)}, u32[]{:S(2)}, u32[]{:S(2)}) collective-permute-start(f32[1,1024]{1,0:T(1,128)S(1)} %relay.15), channel_id=1, source_target_pairs={{0,1},{1,0},{2,3},{3,2},{4,5},{5,4},{6,7},{7,6},{8,9},{9,8},{10,11... | collective-permute-start | bytes 12296 | tf_op jit(solution)/shard_map/ppermute | solution.py:457
  (15 other events, 98.5 us)
